TPU v7x, 32 devices: a whole 2x2x4 slice. The times are simulated.
32 devices in a mesh: dp: 8 (over z, x), tensor: 4 (over y, core).
Axes of the slice: x: 2, y: 2, z: 4, core: 2. Of those that a mesh axis runs over, the one named last changes fastest.
Arguments:
- inputs: bfloat16 [8, 3, 512, 1024], P('dp', None, 'tensor'), may hold values from -6 to 6
- lengths: int32 [8, 3], P('dp'), may hold values from 128 to 512, as said below
- cotangent: bfloat16 [8, 3, 512, 1024], P('dp', None, 'tensor'), may hold values from -6 to 6
- w_qkv: bfloat16 [1024, 3, 1024], P(None, None, 'tensor'), may hold values from -0.1875 to 0.1875
- b_query: bfloat16 [1024], P('tensor'), may hold values from -3 to 3
- b_value: bfloat16 [1024], P('tensor'), may hold values from -3 to 3
- w_out: bfloat16 [1024, 1024], P('tensor'), may hold values from -0.75 to 0.75
- b_out: bfloat16 [1024], replicated, may hold values from -3 to 3
- ln1_gain: bfloat16 [1024], replicated, may hold values from 0.5 to 1.5
- ln1_bias: bfloat16 [1024], replicated, may hold values from -3 to 3
- w_up: bfloat16 [1024, 4096], P(None, 'tensor'), may hold values from -0.1875 to 0.1875
- b_up: bfloat16 [4096], P('tensor'), may hold values from -3 to 3
- w_down: bfloat16 [4096, 1024], P('tensor'), may hold values from -0.09375 to 0.09375
- b_down: bfloat16 [1024], replicated, may hold values from -3 to 3
- ln2_gain: bfloat16 [1024], replicated, may hold values from 0.5 to 1.5
- ln2_bias: bfloat16 [1024], replicated, may hold values from -3 to 3
Outputs:
- output: bfloat16 [8, 3, 512, 1024], P('dp', None, 'tensor')
- grad_inputs: bfloat16 [8, 3, 512, 1024], P('dp', None, 'tensor')
- grad_qkv: float32 [1024, 3, 1024], P(None, None, 'tensor')
- grad_query_bias: float32 [1024], P('tensor')
- grad_value_bias: float32 [1024], P('tensor')
- grad_out: float32 [1024, 1024], P('tensor')
- grad_out_bias: float32 [1024], replicated
- grad_ln1_gain: float32 [1024], replicated
- grad_ln1_bias: float32 [1024], replicated
- grad_up: float32 [1024, 4096], P(None, 'tensor')
- grad_up_bias: float32 [4096], P('tensor')
- grad_down: float32 [4096, 1024], P('tensor')
- grad_down_bias: float32 [1024], replicated
- grad_ln2_gain: float32 [1024], replicated
- grad_ln2_bias: float32 [1024], replicated
Inputs may be any that keep to these rules, and one draw needn't show every extreme that they name: Each row of lengths has one entry equal to 512; a sequence fills the first lengths entries of its 512 slots, the rest is padding.
All inputs are finite; a program needn't handle non-finite values.
Results may differ from a plain program's by a relative error of at most 0.018.
Values may be sent and summed in bfloat16 or wider, within the bound.
A program may use at most 128 MiB of HBM per device.

v0:
```python
import functools

import jax
import jax.numpy as jnp
from jax import lax
from jax.experimental import pallas as pl
from jax.experimental.pallas import tpu as pltpu
from jax.sharding import PartitionSpec as P

HD = 64
EPSILON = 1e-05
F32 = jnp.float32
LOW = jnp.bfloat16
MESH = pl.DeviceIdType.MESH
TILE = 256
PHASES = 4
UNIT = 64


def dot(left, right, left_dim=1, right_dim=0):
    return lax.dot_general(
        left, right, (((left_dim,), (right_dim,)), ((), ())), preferred_element_type=F32
    )


def row_sum(values):
    return jnp.sum(values, axis=0, keepdims=True)


def row_mean(values):
    return jnp.mean(values, axis=-1, keepdims=True)


def gelu_parts(h):
    t = 1.0 / (1.0 + 0.23164188 * jnp.abs(h))
    density = jnp.exp(-0.5 * h * h)
    series = t * (
        0.127414796
        + t * (-0.142248368 + t * (0.7107068705 + t * (-0.7265760135 + t * 0.5307027145)))
    )
    tail = series * density
    return jnp.where(h < 0.0, tail, 1.0 - tail), density * 0.3989422804014327


HOPS = 11
RING = 16
SHORT_RING = 8
STAGE_AT = (0, 1, 2, 3, 4, 6)
STORE_TICKS = 3
TICK = ("tick", 0)
SCHEDULE = (
    ("finish", 5),
    ("gather", 6),
    ("compute", 6),
    ("forward", 7),
    ("send", 6),
    ("gather", 7),
    ("compute", 7),
    ("pass", 6),
    ("forward", 8),
    ("gather", 8),
    TICK,
    ("send", 7),
    ("pass", 7),
    TICK,
    ("finish", 6),
    TICK,
    ("compute", 8),
    *[TICK] * 2,
    ("finish", 7),
    ("send", 8),
    ("forward", 9),
    TICK,
    ("gather", 9),
    ("pass", 8),
    TICK,
    ("compute", 9),
    TICK,
    ("forward", 10),
    TICK,
    ("finish", 8),
    ("send", 9),
    TICK,
    ("gather", 10),
    ("pass", 9),
    TICK,
    ("compute", 10),
    ("send", 10),
    TICK,
    ("forward", 11),
    ("pass", 10),
    TICK,
    ("gather", 11),
    ("compute", 11),
    TICK,
    ("send", 11),
    TICK,
    ("pass", 11),
    *[TICK] * 4,
    ("finish", 9),
    ("finish", 10),
    *[TICK] * 2,
    ("finish", 11),
    TICK,
)


class Reducer:
    def __init__(self, gb, rx, rz, rm, rb, rn, rq, send_sems, recv_sems):
        dp = lax.axis_index("dp")
        self.x = lax.rem(dp, 2)
        self.z = lax.div(dp, 2)
        self.side = lax.rem(self.z, 2)
        self.m = lax.div(self.z, 2)
        self.inner = self.side != self.m
        self.outer = self.side == self.m
        self.to_x = {"dp": self.z * 2 + (1 - self.x)}
        self.to_pair = {"dp": (self.z + 1 - 2 * self.side) * 2 + self.x}
        self.to_mid = {"dp": (3 - self.z) * 2 + self.x}
        self.gb, self.rx, self.rz, self.rm, self.rb, self.rn, self.rq = gb, rx, rz, rm, rb, rn, rq
        self.send_sems, self.recv_sems = send_sems, recv_sems

    def greet(self, extra=()):
        barrier = pltpu.get_barrier_semaphore()

        def signal(device):
            pl.semaphore_signal(barrier, inc=1, device_id=device, device_id_type=MESH)

        for device in (self.to_x, self.to_pair) + tuple(extra):
            signal(device)

        @pl.when(self.inner)
        def _():
            signal(self.to_mid)
            pl.semaphore_wait(barrier, 3 + len(extra))

        @pl.when(self.outer)
        def _():
            pl.semaphore_wait(barrier, 2 + len(extra))

    def copy(self, hop, k, src, dst, device):
        return pltpu.make_async_remote_copy(
            src_ref=src,
            dst_ref=dst,
            send_sem=self.send_sems.at[hop, k],
            recv_sem=self.recv_sems.at[hop, k],
            device_id=device,
            device_id_type=MESH,
        )

    def ax(self, k):
        return self.copy(0, k, self.gb.at[2 * k, 1 - self.x], self.rx.at[k % RING, 1 - self.x], self.to_x)

    def az(self, k):
        return self.copy(1, k, self.gb.at[2 * k, self.x], self.rz.at[k % SHORT_RING], self.to_pair)

    def am(self, k):
        return self.copy(2, k, self.gb.at[2 * k, self.x], self.rm.at[k % SHORT_RING], self.to_mid)

    def ao(self, k):
        return self.copy(3, k, self.rx.at[k % RING, self.x], self.rx.at[k % RING, self.x], self.to_pair)

    def ag(self, k):
        return self.copy(4, k, self.rx.at[k % RING, self.x], self.rx.at[k % RING, self.x], self.to_x)

    def bi(self, k):
        return self.copy(5, k, self.gb.at[2 * k + 1], self.rb.at[k % RING], self.to_pair)

    def bm(self, k):
        return self.copy(6, k, self.gb.at[2 * k + 1, 1 - self.m], self.rn.at[k % SHORT_RING], self.to_mid)

    def bx(self, k):
        return self.copy(7, k, self.gb.at[2 * k + 1, self.m], self.rq.at[k % SHORT_RING], self.to_x)

    def bg(self, k):
        return self.copy(8, k, self.rb.at[k % RING, self.m], self.rb.at[k % RING, self.m], self.to_mid)

    def bo(self, k):
        return self.copy(9, k, self.rb.at[k % RING, self.m], self.rb.at[k % RING, self.m], self.to_pair)

    def bp(self, k):
        return self.copy(10, k, self.rb.at[k % RING, 1 - self.m], self.rb.at[k % RING, 1 - self.m], self.to_pair)

    def add(self, out, left, right):
        out[...] = (left[...].astype(F32) + right[...].astype(F32)).astype(LOW)

    def start(self, k):
        self.ax(k).start()

        @pl.when(self.outer)
        def _():
            self.bi(k).start()

    def stage1(self, k):
        self.ax(k).wait()
        own = self.gb.at[2 * k, self.x]
        self.add(own, own, self.rx.at[k % RING, self.x])

        @pl.when(self.outer)
        def _():
            self.az(k).start()

    def stage2(self, k):
        @pl.when(self.inner)
        def _():
            self.bi(k).wait_recv()
            away = self.gb.at[2 * k + 1, 1 - self.m]
            self.add(away, away, self.rb.at[k % RING, 1 - self.m])
            self.bm(k).start()
            own = self.gb.at[2 * k + 1, self.m]
            self.add(own, own, self.rb.at[k % RING, self.m])
            self.az(k).wait_recv()
            own = self.gb.at[2 * k, self.x]
            self.add(own, own, self.rz.at[k % SHORT_RING])
            self.am(k).start()

    def stage3(self, k):
        @pl.when(self.inner)
        def _():
            self.bm(k).wait()
            own = self.gb.at[2 * k + 1, self.m]
            self.add(own, own, self.rn.at[k % SHORT_RING])
            self.bx(k).start()
            self.am(k).wait()
            self.add(self.rx.at[k % RING, self.x], self.gb.at[2 * k, self.x], self.rm.at[k % SHORT_RING])
            self.ao(k).start()
            self.ag(k).start()

    def stage4(self, k):
        @pl.when(self.inner)
        def _():
            self.bx(k).wait()
            self.add(self.rb.at[k % RING, self.m], self.gb.at[2 * k + 1, self.m], self.rq.at[k % SHORT_RING])
            self.bg(k).start()
            self.bo(k).start()

        @pl.when(self.outer)
        def _():
            self.ao(k).wait_recv()
            self.ag(k).start()

    def stage5(self, k):
        @pl.when(self.inner)
        def _():
            self.bg(k).wait_recv()
            self.bp(k).start()

        self.ag(k).wait_recv()

    def stage6(self, k):
        @pl.when(self.outer)
        def _():
            self.bo(k).wait_recv()
            self.bp(k).wait_recv()

    def drain(self, k):
        self.ag(k).wait_send()

        @pl.when(self.inner)
        def _():
            self.ao(k).wait_send()
            self.bg(k).wait_send()
            self.bo(k).wait_send()
            self.bp(k).wait_send()

        @pl.when(self.outer)
        def _():
            self.az(k).wait_send()
            self.bi(k).wait_send()

    stages = (stage1, stage2, stage3, stage4, stage5, stage6)


VECTOR_HOPS = 6


class VectorReducer:
    def __init__(self, reducer, held, landed, send_sem, recv_sem, shared):
        t = lax.axis_index("tensor")
        c = lax.rem(t, 2)
        y = lax.div(t, 2)
        self.r = reducer
        self.held, self.landed, self.send_sem, self.recv_sem = held, landed, send_sem, recv_sem
        self.shared = shared
        self.devices = (
            {"tensor": y * 2 + (1 - c)},
            {"tensor": (1 - y) * 2 + c},
            reducer.to_x,
            reducer.to_pair,
            reducer.to_mid,
            reducer.to_pair,
        )

    def copy(self, hop):
        src = self.held.at[5 if hop == 5 else hop]
        dst = self.held.at[5] if hop == 5 else self.landed.at[hop]
        return pltpu.make_async_remote_copy(
            src_ref=src,
            dst_ref=dst,
            send_sem=self.send_sem.at[hop],
            recv_sem=self.recv_sem.at[hop],
            device_id=self.devices[hop],
            device_id_type=MESH,
        )

    def begin(self, hop):
        if hop < 3:
            self.copy(hop).start()
        else:

            @pl.when(self.r.outer if hop == 3 else self.r.inner)
            def _():
                self.copy(hop).start()

    def end(self, hop):
        if hop < 3:
            self.copy(hop).wait()
            got = self.landed[hop]
            if hop < 2:
                row = lax.broadcasted_iota(jnp.int32, got.shape, 0)
                got = jnp.where(row < self.shared, got, 0.0)
            self.held[hop + 1] = self.held[hop] + got
        elif hop == 3:

            @pl.when(self.r.outer)
            def _():
                self.copy(3).wait_send()

            @pl.when(self.r.inner)
            def _():
                self.copy(3).wait_recv()
                self.held[4] = self.held[3] + self.landed[3]

        elif hop == 4:

            @pl.when(self.r.inner)
            def _():
                self.copy(4).wait()
                self.held[5] = self.held[4] + self.landed[4]

        else:

            @pl.when(self.r.inner)
            def _():
                self.copy(5).wait_send()

            @pl.when(self.r.outer)
            def _():
                self.copy(5).wait_recv()


def layer_kernel(
    lengths_ref,
    x_ref,
    cot_ref,
    wqkv_ref,
    wout_ref,
    wup_ref,
    wdown_ref,
    bout_ref,
    gain1_ref,
    bias1_ref,
    bdown_ref,
    gain2_ref,
    bias2_ref,
    bup_ref,
    bquery_ref,
    bvalue_ref,
    out_ref,
    gin_ref,
    gdown_ref,
    gup_ref,
    gout_ref,
    gqkv_ref,
    vsum_ref,
    xa,
    wq,
    wo,
    wu,
    wd,
    qkv,
    pt,
    cc,
    ua,
    act,
    gp,
    g2a,
    g1a,
    part,
    rc,
    ys,
    ry,
    xh1,
    rstd1,
    resid,
    cot,
    gb,
    rx,
    rz,
    rm,
    rb,
    rn,
    rq,
    held,
    landed,
    vg,
    vec_ref,
    grads,
    load_sem,
    store_sem,
    agy_send,
    agy_recv,
    agc_send,
    agc_recv,
    agf_send,
    agf_recv,
    rsc_send,
    rsc_recv,
    rsy_send,
    rsy_recv,
    hop_send,
    hop_recv,
    vec_send,
    vec_recv,
    grad_sem,
    *,
    summed,
):
    batches = x_ref.shape[0]
    block = x_ref.shape[1]
    width = x_ref.shape[2]
    head_cols = wo.shape[0]
    hidden = wu.shape[1]
    rows = 4 * block
    pairs = head_cols // 128
    t = lax.axis_index("tensor")
    c = lax.rem(t, 2)
    y = lax.div(t, 2)
    t_core = y * 2 + (1 - c)
    t_y = (1 - y) * 2 + c
    t_far = (1 - y) * 2 + (1 - c)
    core = {"tensor": t_core}
    across = {"tensor": t_y}

    gathers = (xa, ua, g2a, g1a)

    def remote(src, dst, send, recv, device):
        return pltpu.make_async_remote_copy(
            src_ref=src, dst_ref=dst, send_sem=send, recv_sem=recv, device_id=device, device_id_type=MESH
        )

    def ag_y(p, s, at, src=None):
        buf = gathers[p]
        return remote(
            buf.at[s, at] if src is None else src, buf.at[s, at], agy_send.at[p, s], agy_recv.at[p, s], across
        )

    def ag_c(p, s, at, src=None):
        buf = gathers[p]
        return remote(
            buf.at[s, at] if src is None else src, buf.at[s, at], agc_send.at[p, s], agc_recv.at[p, s], core
        )

    def ag_f(p, s, at):
        buf = gathers[p]
        return remote(buf.at[s, at], buf.at[s, at], agf_send.at[p, s], agf_recv.at[p, s], core)

    def rs_c(p, s):
        return remote(part.at[s, 1 - c], rc.at[s], rsc_send.at[p, s], rsc_recv.at[p, s], core)

    def rs_y(p, s):
        return remote(ys.at[s], ry.at[s], rsy_send.at[p, s], rsy_recv.at[p, s], across)

    def load(index, src, dst):
        return pltpu.make_async_copy(src, dst, load_sem.at[index])

    def store(index, src, dst):
        return pltpu.make_async_copy(src, dst, store_sem.at[index])

    loads = [load(s, x_ref.at[s], xa.at[s, t]) for s in range(batches)]
    n = batches
    load_wq = load(n, wqkv_ref, wq)
    load_wo = load(n + 1, wout_ref, wo)
    load_wu = load(n + 2, wup_ref, wu)
    load_wd = load(n + 3, wdown_ref, wd)
    load_cot = load(n + 4, cot_ref, cot)

    for cp in loads:
        cp.start()
    if summed:
        reducer = Reducer(gb, rx, rz, rm, rb, rn, rq, hop_send, hop_recv)
        vectors = VectorReducer(reducer, held, landed, vec_send, vec_recv, 6)
        reducer.greet((core, across))
    else:
        barrier = pltpu.get_barrier_semaphore()
        for device in (core, across):
            pl.semaphore_signal(barrier, inc=1, device_id=device, device_id_type=MESH)
        pl.semaphore_wait(barrier, 2)
    for s in range(batches):
        ag_y(0, s, t, x_ref.at[s]).start()
        ag_c(0, s, t, x_ref.at[s]).start()
    load_wq.start()
    load_wo.start()
    load_wu.start()
    load_wd.start()
    load_cot.start()

    vg[...] = jnp.zeros_like(vg)
    long_refs = (bout_ref, gain1_ref, bias1_ref, bdown_ref, gain2_ref, bias2_ref, bup_ref)
    for i, ref in enumerate(long_refs):
        vec_ref[i : i + 1, :] = ref[...].astype(F32).reshape(1, -1)
    for i, ref in enumerate((bquery_ref, bvalue_ref)):
        vec_ref[7:8, i * head_cols : (i + 1) * head_cols] = ref[...].astype(F32).reshape(1, -1)
    lane = lax.broadcasted_iota(jnp.int32, (rows, 128), 1)
    low_half = lane < HD
    empty = jnp.zeros((rows, 128), LOW)

    def masked(values, h):
        return jnp.where(low_half, values, empty) if h == 0 else jnp.where(low_half, empty, values)

    def vec(i):
        return vec_ref[i : i + 1, :]

    def whole(ref, s):
        return ref[s].reshape(rows, width)

    def put_part(s, j, values):
        values = values.astype(LOW)
        cols = pl.ds(pl.multiple_of(j * TILE, TILE), TILE)
        for b in range(4):
            part[s, b % 2, b // 2, :, cols] = values[b * block : (b + 1) * block]

    def compute_a(s):
        tokens = whole(xa, s)
        q = dot(tokens, wq[0]) + vec_ref[7:8, :head_cols]
        qkv[s, 0] = q.astype(LOW) * LOW(HD ** (-0.5))
        qkv[s, 1] = dot(tokens, wq[1]).astype(LOW)
        v = dot(tokens, wq[2]) + vec_ref[7:8, head_cols : 2 * head_cols]
        qkv[s, 2] = v.astype(LOW)
        keys_valid = lax.broadcasted_iota(jnp.int32, (rows, rows), 0) < lengths_ref[0, s]
        for j in range(pairs):
            cols = slice(j * 128, (j + 1) * 128)
            q, k, v = qkv[s, 0, :, cols], qkv[s, 1, :, cols], qkv[s, 2, :, cols]
            context = jnp.zeros((128, rows), F32)
            for h in range(2):
                scores = dot(k, masked(q, h), 1, 1)
                scores = jnp.where(keys_valid, scores, -1e30)
                weights = jnp.exp(scores - jnp.max(scores, axis=0, keepdims=True))
                p = (weights * (1.0 / row_sum(weights))).astype(LOW)
                pt[s, 2 * j + h] = p
                context = context + dot(masked(v, h).T, p)
            cc[s, :, cols] = context.T.astype(LOW)
        context = cc[s]
        for j in range(width // TILE):
            put_part(s, j, dot(context, wo[:, j * TILE : (j + 1) * TILE]))

    def compute_c(s):
        normed = whole(ua, s)
        for j in range(hidden // TILE):
            cols = slice(j * TILE, (j + 1) * TILE)
            h = dot(normed, wu[:, cols]) + vec_ref[6:7, cols]
            phi, density = gelu_parts(h)
            act[s, :, cols] = (h * phi).astype(LOW)
            gp[s, :, cols] = (phi + h * density).astype(LOW)
        activated = act[s]
        for j in range(width // TILE):
            put_part(s, j, dot(activated, wd[:, j * TILE : (j + 1) * TILE]))

    def compute_e(s):
        def tile(j, carry):
            cols = pl.ds(pl.multiple_of(j * TILE, TILE), TILE)
            gh = gp[s, :, cols].astype(F32) * dot(whole(g2a, s), wd[cols, :], 1, 1)
            vg[6:7, cols] += row_sum(gh)
            gp[s, :, cols] = gh.astype(LOW)
            return carry

        lax.fori_loop(0, hidden // TILE, tile, 0)

        def back(j, carry):
            rows_at = pl.ds(pl.multiple_of(j * TILE, TILE), TILE)
            put_part(s, j, dot(gp[s], wu[rows_at, :], 1, 1))
            return carry

        lax.fori_loop(0, width // TILE, back, 0)

    def compute_g(s):
        grads[...] = dot(whole(g1a, s), wo[...], 1, 1).astype(LOW)

        def pair(j, carry):
            cols = pl.ds(pl.multiple_of(j * 128, 128), 128)
            q, k, v = qkv[s, 0, :, cols], qkv[s, 1, :, cols], qkv[s, 2, :, cols]
            gc = grads[:, cols]
            dq = jnp.zeros((128, rows), F32)
            dk = jnp.zeros((rows, 128), F32)
            dv = jnp.zeros((rows, 128), F32)
            for h in range(2):
                gc_h = masked(gc, h)
                p = pt[s, 2 * j + h]
                wide = p.astype(F32)
                product = wide * dot(v, gc_h, 1, 1)
                ds = (product - wide * row_sum(product)).astype(LOW)
                dv = dv + dot(p, gc_h)
                dk = dk + dot(ds, masked(q, h))
                dq = dq + dot(masked(k, h).T, ds)
            dq = dq.T * (HD ** (-0.5))
            vg[7:8, cols] += row_sum(dq)
            vg[7:8, pl.ds(pl.multiple_of(head_cols + j * 128, 128), 128)] += row_sum(dv)
            qkv[s, 0, :, cols] = dq.astype(LOW)
            qkv[s, 1, :, cols] = dk.astype(LOW)
            qkv[s, 2, :, cols] = dv.astype(LOW)
            return carry

        lax.fori_loop(0, pairs, pair, 0)

        def back(j, carry):
            at = pl.ds(pl.multiple_of(j * TILE, TILE), TILE)
            total = dot(qkv[s, 0], wq[0, at, :], 1, 1)
            total = total + dot(qkv[s, 1], wq[1, at, :], 1, 1)
            total = total + dot(qkv[s, 2], wq[2, at, :], 1, 1)
            put_part(s, j, total)
            return carry

        lax.fori_loop(0, width // TILE, back, 0)

    computes = (compute_a, compute_c, compute_e, compute_g)

    def reduced(p, s):
        rs_y(p, s).wait()
        rs_c(p, s).wait_send()
        return part[s, c, y].astype(F32) + rc[s, y].astype(F32) + ry[s].astype(F32)

    def send_on(p, s):
        ag_y(p, s, t).start()
        ag_c(p, s, t).start()

    def finish_a(s):
        z = xa[s, t].astype(F32) + (reduced(0, s) + vec(0))
        centred = z - row_mean(z)
        rstd = lax.rsqrt(row_mean(centred * centred) + EPSILON)
        hat = centred * rstd
        xh1[s] = hat
        rstd1[s] = jnp.broadcast_to(rstd, rstd1.shape[1:])
        ua[s, t] = (hat * vec(1) + vec(2)).astype(LOW)
        send_on(1, s)

    def finish_c(s):
        z = (xh1[s] * vec(1) + vec(2)) + (reduced(1, s) + vec(3))
        centred = z - row_mean(z)
        rstd = lax.rsqrt(row_mean(centred * centred) + EPSILON)
        hat = centred * rstd
        valid = t * block + lax.broadcasted_iota(jnp.int32, (block, width), 0) < lengths_ref[0, s]
        incoming = jnp.where(valid, cot[s].astype(F32), 0.0)
        scaled = incoming * vec(4)
        grad = rstd * (scaled - row_mean(scaled) - hat * row_mean(scaled * hat))
        resid[s] = grad
        g2a[s, t] = grad.astype(LOW)
        send_on(2, s)
        cot[s] = jnp.where(valid, hat * vec(4) + vec(5), 0.0).astype(LOW)
        store(s, cot.at[s], out_ref.at[s]).start()
        vg[3:4, :] += row_sum(grad)
        vg[4:5, :] += row_sum(incoming * hat)
        vg[5:6, :] += row_sum(incoming)

    def finish_e(s):
        gu = resid[s] + reduced(2, s)
        hat = xh1[s]
        scaled = gu * vec(1)
        grad = rstd1[s, :, :1] * (scaled - row_mean(scaled) - hat * row_mean(scaled * hat))
        resid[s] = grad
        g1a[s, t] = grad.astype(LOW)
        send_on(3, s)
        vg[0:1, :] += row_sum(grad)
        vg[1:2, :] += row_sum(gu * hat)
        vg[2:3, :] += row_sum(gu)

    def finish_g(s):
        store(s, cot.at[s], out_ref.at[s]).wait()
        cot[s] = (resid[s] + reduced(3, s)).astype(LOW)
        store(batches + s, cot.at[s], gin_ref.at[s]).start()

    finishes = (finish_a, finish_c, finish_e, finish_g)

    def forward_block(p, s):
        ag_y(p, s, t_y).wait_recv()
        ag_f(p, s, t_y).start()

    def gathered(p, s):
        ag_c(p, s, t_core).wait_recv()
        ag_f(p, s, t_far).wait_recv()

    def send_sums(p, s):
        rs_c(p, s).start()

    def pass_sums(p, s):
        rs_c(p, s).wait_recv()
        ys[s] = (part[s, c, 1 - y].astype(F32) + rc[s, 1 - y].astype(F32)).astype(LOW)
        rs_y(p, s).start()

    def tall(values):
        return values.reshape(batches * rows, -1)

    per_piece = TILE // UNIT
    down_pieces = hidden // TILE
    up_pieces = width // TILE
    early_pieces = down_pieces + up_pieces
    pieces = early_pieces + 1 + 3

    def piece(d):
        if d < down_pieces:
            cols = slice(d * TILE, (d + 1) * TILE)
            product = dot(tall(act[:, :, cols]), tall(g2a[...]), 0, 0)
        elif d < early_pieces:
            cols = slice((d - down_pieces) * TILE, (d - down_pieces + 1) * TILE)
            product = dot(tall(ua[:, :, :, cols]), tall(gp[...]), 0, 0)
        elif d == early_pieces:
            product = dot(tall(cc[...]), tall(g1a[...]), 0, 0)
        else:
            right = tall(qkv[:, d - early_pieces - 1])
            for j in range(per_piece):
                cols = slice(j * TILE, (j + 1) * TILE)
                product = dot(tall(xa[:, :, :, cols]), right, 0, 0).astype(LOW)
                for h in range(per_piece):
                    gb[d * per_piece + j, :, :, h * head_cols : (h + 1) * head_cols] = product[
                        h * UNIT : (h + 1) * UNIT
                    ].reshape(2, UNIT // 2, head_cols)
            return
        product = product.astype(LOW)
        for u in range(per_piece):
            gb[d * per_piece + u] = product[u * UNIT : (u + 1) * UNIT].reshape(2, UNIT // 2, width)

    def unit_stores(i, src):
        def make(n, src, dst):
            return pltpu.make_async_copy(src, dst, grad_sem.at[i, n])

        if i < down_pieces * per_piece:
            return [make(0, src, gdown_ref.at[i])]
        i_up = i - down_pieces * per_piece
        if i_up < up_pieces * per_piece:
            return [make(0, src, gup_ref.at[i_up])]
        i_out = i - early_pieces * per_piece
        if i_out < per_piece:
            return [make(0, src, gout_ref.at[i_out])]
        i_qkv = i_out - per_piece
        kind, j = i_qkv // per_piece, i_qkv % per_piece
        return [
            make(h, src.at[:, :, pl.ds(h * head_cols, head_cols)], gqkv_ref.at[kind, j * per_piece + h])
            for h in range(per_piece)
        ]

    unit_pairs = pieces * per_piece // 2

    def pair_stores(k):
        return unit_stores(2 * k, rx.at[k % RING]) + unit_stores(2 * k + 1, rb.at[k % RING])

    ticks = iter(range(-1, unit_pairs + STAGE_AT[-1] + STORE_TICKS + 1))

    def tick():
        now = next(ticks, None)
        if now is None:
            return False
        if 0 <= now - STAGE_AT[-1] - STORE_TICKS < unit_pairs:
            reducer.drain(now - STAGE_AT[-1] - STORE_TICKS)
            for cp in pair_stores(now - STAGE_AT[-1] - STORE_TICKS):
                cp.wait()
        k = now + 1
        if k < unit_pairs:
            if 2 * k % per_piece == 0:
                piece(2 * k // per_piece)
            reducer.start(k)
        for stage, at in zip(reducer.stages, STAGE_AT):
            if 0 <= now - at < unit_pairs:
                stage(reducer, now - at)
        if 0 <= now - STAGE_AT[-1] < unit_pairs:
            for cp in pair_stores(now - STAGE_AT[-1]):
                cp.start()
        return True

    def step(s, carry, p):
        gathered(p, s)
        computes[p](s)
        send_sums(p, s)
        pass_sums(p, s)
        if p > 0:

            @pl.when(s == 0)
            def _():
                finishes[p - 1](batches - 1)

        @pl.when(s > 0)
        def _():
            finishes[p](s - 1)

        @pl.when(s < batches - 1)
        def _():
            forward_block(p, s + 1)

        @pl.when(s == batches - 1)
        def _():
            forward_block(p + 1, 0)

        return carry

    forward_block(0, 0)
    for cp in loads:
        cp.wait()
    load_wq.wait()
    load_wo.wait()
    lax.fori_loop(0, batches, functools.partial(step, p=0), 0)
    load_wu.wait()
    load_wd.wait()
    load_cot.wait()
    lax.fori_loop(0, batches, functools.partial(step, p=1), 0)

    hops = iter(range(VECTOR_HOPS + 1))

    def vector_hop():
        hop = next(hops, None)
        if hop is None:
            return False
        if hop == 0:
            held[0] = vg[...]
        else:
            vectors.end(hop - 1)
        if hop < VECTOR_HOPS:
            vectors.begin(hop)
        return True

    actions = {
        "gather": gathered,
        "compute": lambda p, s: computes[p](s),
        "send": send_sums,
        "pass": pass_sums,
        "finish": lambda p, s: finishes[p](s),
        "forward": forward_block,
    }
    last = PHASES * batches - 1
    vectors_wait = {("compute", last), ("finish", last - 1)}
    for action in SCHEDULE:
        if action == TICK:
            if summed:
                if not vectors_wait:
                    vector_hop()
                tick()
        else:
            name, index = action
            actions[name](index // batches, index % batches)
            vectors_wait.discard(action)
    if summed:
        while tick():
            vector_hop()
        while vector_hop():
            pass
        vsum_ref[...] = held[VECTOR_HOPS - 1]
    else:
        stores = []
        for d in range(pieces):
            piece(d)
            for i in range(d * per_piece, (d + 1) * per_piece):
                stores += unit_stores(i, gb.at[i])
                for cp in unit_stores(i, gb.at[i]):
                    cp.start()
        vsum_ref[...] = vg[...]
        for cp in stores:
            cp.wait()
    for s in range(batches):
        store(batches + s, cot.at[s], gin_ref.at[s]).wait()

    def drain(i, carry):
        for p in range(PHASES):
            ag_y(p, i, t).wait_send()
            ag_c(p, i, t).wait_send()
            ag_f(p, i, t_y).wait_send()
        return carry

    lax.fori_loop(0, batches, drain, 0)


def run_layer(lengths, x, cot, wqkv, wout, wup, wdown, vectors, summed):
    batches, block, width = x.shape
    rows = 4 * block
    head_cols = wout.shape[0]
    heads = head_cols // HD
    hidden = wup.shape[1]
    half = UNIT // 2
    down, up, out = hidden // UNIT, width // UNIT, head_cols // UNIT
    units = down + up + out + 3 * out
    ring, short_ring = (RING, SHORT_RING) if summed else (1, 1)
    any_space = pl.BlockSpec(memory_space=pl.ANY)
    vmem = pl.BlockSpec(memory_space=pltpu.VMEM)
    dma = pltpu.SemaphoreType.DMA
    low = lambda *shape: pltpu.VMEM(shape, LOW)
    wide = lambda *shape: pltpu.VMEM(shape, F32)
    gathered = low(batches, 4, block, width)
    scratch = [
        gathered,
        low(3, width, head_cols),
        low(head_cols, width),
        low(width, hidden),
        low(hidden, width),
        low(batches, 3, rows, head_cols),
        low(batches, heads, rows, rows),
        low(batches, rows, head_cols),
        gathered,
        low(batches, rows, hidden),
        low(batches, rows, hidden),
        gathered,
        gathered,
        low(batches, 2, 2, block, width),
        low(batches, 2, block, width),
        low(batches, block, width),
        low(batches, block, width),
        wide(batches, block, width),
        wide(batches, block, 128),
        wide(batches, block, width),
        low(batches, block, width),
        low(units, 2, half, width),
        low(ring, 2, half, width),
        low(short_ring, half, width),
        low(short_ring, half, width),
        low(ring, 2, half, width),
        low(short_ring, half, width),
        low(short_ring, half, width),
        wide(VECTOR_HOPS, 8, width),
        wide(VECTOR_HOPS - 1, 8, width),
        wide(8, width),
        wide(8, width),
        low(rows, head_cols),
        dma((batches + 5,)),
        dma((2 * batches,)),
    ]
    scratch += [dma((PHASES, batches))] * 10 + [dma((HOPS, units // 2))] * 2 + [dma((VECTOR_HOPS,))] * 2
    scratch.append(dma((units, TILE // UNIT)))
    low_out = lambda *shape: jax.ShapeDtypeStruct(shape, LOW)
    return pl.pallas_call(
        functools.partial(layer_kernel, summed=summed),
        out_shape=(
            low_out(batches, block, width),
            low_out(batches, block, width),
            low_out(down, 2, half, width),
            low_out(up, 2, half, hidden),
            low_out(out, 2, half, width),
            low_out(3, width // UNIT, 2, half, head_cols),
            jax.ShapeDtypeStruct((8, width), F32),
        ),
        in_specs=[pl.BlockSpec(memory_space=pltpu.SMEM)] + [any_space] * 6 + [vmem] * 9,
        out_specs=(any_space,) * 6 + (vmem,),
        scratch_shapes=scratch,
        compiler_params=pltpu.CompilerParams(
            collective_id=0, has_side_effects=True, vmem_limit_bytes=63 << 20
        ),
        name="layer",
    )(lengths, x, cot, wqkv, wout, wup, wdown, *vectors)


def widen_kernel(
    down_ref, up_ref, out_ref, qkv_ref, sums_ref, rows_ref, gin_ref,
    down_wide, up_wide, out_wide, qkv_wide, *refs,
):
    vectors, (rows_copy, gin_copy, low, wide, low_qkv, wide_qkv, rows, load_sem, store_sem) = refs[:9], refs[9:]
    work = []

    def part(src, dst, held, made):
        n = len(work)
        get = pltpu.make_async_copy(src, held, load_sem.at[n])
        put = pltpu.make_async_copy(made, dst, store_sem.at[n])
        work.append((get, held, made, put))

    i = 0
    for src, dst in ((down_ref, down_wide), (up_ref, up_wide), (out_ref, out_wide)):
        for at in range(0, src.shape[0], TILE):
            part(src.at[pl.ds(at, TILE)], dst.at[pl.ds(at, TILE)], low.at[i], wide.at[i])
            i += 1
    for i in range(3):
        part(qkv_ref.at[i], qkv_wide.at[i], low_qkv.at[i], wide_qkv.at[i])
    for i, (src, dst) in enumerate(((rows_ref, rows_copy), (gin_ref, gin_copy))):
        block = rows.at[i]
        part(src, dst, block, block)
    for get, _, _, _ in work:
        get.start()
    head_cols = vectors[0].shape[0]
    vectors[0][...] = sums_ref[7, :head_cols]
    vectors[1][...] = sums_ref[7, head_cols : 2 * head_cols]
    for ref, row in zip(vectors[2:], (0, 1, 2, 6, 3, 4, 5)):
        ref[...] = sums_ref[row]
    for get, held, made, put in work:
        get.wait()
        if made is not held:
            made[...] = held[...].astype(F32)
        put.start()
    for _, _, _, put in work:
        put.wait()


def widen(down, up, out, qkv, sums, rows, gin):
    any_space = pl.BlockSpec(memory_space=pl.ANY)
    vmem = pl.BlockSpec(memory_space=pltpu.VMEM)
    dma = pltpu.SemaphoreType.DMA
    width = down.shape[1]
    pieces = (down.shape[0] + up.shape[0] + out.shape[0]) // TILE
    as_wide = lambda a: jax.ShapeDtypeStruct(a.shape, F32)
    vector = lambda n: jax.ShapeDtypeStruct((n,), F32)
    return pl.pallas_call(
        widen_kernel,
        out_shape=(
            *map(as_wide, (down, up, out, qkv)),
            *[vector(out.shape[0])] * 2,
            *[vector(width)] * 7,
            jax.ShapeDtypeStruct(rows.shape, rows.dtype),
            jax.ShapeDtypeStruct(gin.shape, gin.dtype),
        ),
        in_specs=[any_space] * 4 + [vmem] + [any_space] * 2,
        out_specs=(any_space,) * 4 + (vmem,) * 9 + (any_space,) * 2,
        scratch_shapes=[
            pltpu.VMEM((pieces, TILE, width), LOW),
            pltpu.VMEM((pieces, TILE, width), F32),
            pltpu.VMEM(qkv.shape, LOW),
            pltpu.VMEM(qkv.shape, F32),
            pltpu.VMEM((2, *rows.shape), LOW),
            dma((pieces + 5,)),
            dma((pieces + 5,)),
        ],
        compiler_params=pltpu.CompilerParams(vmem_limit_bytes=62 << 20),
        name="widen",
    )(down, up, out, qkv, sums, rows, gin)


def per_device(
    inputs,
    lengths,
    cotangent,
    w_qkv,
    b_query,
    b_value,
    w_out,
    b_out,
    ln1_gain,
    ln1_bias,
    w_up,
    b_up,
    w_down,
    b_down,
    ln2_gain,
    ln2_bias,
):
    width = inputs.shape[3]
    head_cols = w_out.shape[0]
    hidden = w_up.shape[1]
    summed = lax.axis_size("dp") == 8
    output, grad_inputs, grad_down, grad_up, grad_out, grad_qkv, sums = run_layer(
        lengths,
        inputs[0],
        cotangent[0],
        jnp.transpose(w_qkv, (1, 0, 2)),
        w_out,
        w_up,
        w_down,
        (b_out, ln1_gain, ln1_bias, b_down, ln2_gain, ln2_bias, b_up, b_query, b_value),
        summed,
    )
    if not summed:
        grad_down, grad_up, grad_out, grad_qkv, sums = lax.psum(
            (grad_down, grad_up, grad_out, grad_qkv, sums), "dp"
        )
        sums = jnp.concatenate([lax.psum(sums[:6], "tensor"), sums[6:]])
    grad_down, grad_up, grad_out, grad_qkv, *rest = widen(
        grad_down.reshape(hidden, width),
        grad_up.reshape(width, hidden),
        grad_out.reshape(head_cols, width),
        grad_qkv.reshape(3, width, head_cols),
        sums,
        output,
        grad_inputs,
    )
    gquery, gvalue, gbout, ggain1, gbias1, gbup, gbdown, ggain2, gbias2, output, grad_inputs = rest
    return (
        output[None],
        grad_inputs[None],
        jnp.transpose(grad_qkv, (1, 0, 2)),
        gquery,
        gvalue,
        grad_out,
        gbout,
        ggain1,
        gbias1,
        grad_up,
        gbup,
        grad_down,
        gbdown,
        ggain2,
        gbias2,
    )


def solution(mesh):
    return jax.shard_map(
        per_device,
        mesh=mesh,
        in_specs=(
            P("dp", None, "tensor", None),
            P("dp", None),
            P("dp", None, "tensor", None),
            P(None, None, "tensor"),
            P("tensor"),
            P("tensor"),
            P("tensor", None),
            P(),
            P(),
            P(),
            P(None, "tensor"),
            P("tensor"),
            P("tensor", None),
            P(),
            P(),
            P(),
        ),
        out_specs=(
            P("dp", None, "tensor", None),
            P("dp", None, "tensor", None),
            P(None, None, "tensor"),
            P("tensor"),
            P("tensor"),
            P("tensor", None),
            P(),
            P(),
            P(),
            P(None, "tensor"),
            P("tensor"),
            P("tensor", None),
            P(),
            P(),
            P(),
        ),
        check_vma=False,
    )
```

profile of v0, /device:TPU:0, one launch (start us, length us, event | category | flops | bytes accessed | tf_op | source)
XLA Modules:
  0.0 240.1 jit_solution(12948406072791772139)
XLA Ops:
  0.7 230.6 %layer.1 = (bf16[3,128,1024]{2,1,0:T(8,128)(2,1)}, bf16[3,128,1024]{2,1,0:T(8,128)(2,1)}, bf16[16,2,32,1024]{3,2,1,0:T(8,128)(2,1)}, bf16[16,2,32,1024]{3,2,1,0:...) custom-call(s32[1,3]{1,0:T(1,128)} %lengths_ref.1, ...), custom_call_target="tpu_custom_call" | custom-call | tf_op jit(solution)/shard_map/layer/pallas_call | solution.py:934
  231.2 8.7 %widen.1 = (f32[1024,1024]{1,0:T(8,128)}, f32[1024,1024]{1,0:T(8,128)}, f32[256,1024]{1,0:T(8,128)}, f32[3,1024,256]{2,1,0:T(8,128)}, f32[256]{0:T(256)}, /*inde...) custom-call(bf16[1024,1024]{1,0:T(8,128)(2,1)} %bitcast.10, ...), custom_call_target="tpu_custom_call" | custom-call | tf_op jit(solution)/shard_map/widen/pallas_call | solution.py:1002
where the time goes:
time: 240 us
  Pallas kernels  239 us (100%)
    pallas_call x1, Pallas kernels, run_layer(): pl.pallas_call(functools.partial(layer_kernel, summed=summed), out_shape=...  231 us
    pallas_call x1, Pallas kernels, widen(): pl.pallas_call(widen_kernel, out_shape=(*map(as_wide, (down, up, out, qkv...  8.65 us

commit v1 on v0

--- a/solution.py
+++ b/solution.py
@@ -49,59 +49,76 @@
 STORE_TICKS = 3
 TICK = ("tick", 0)
 SCHEDULE = (
+    ("gather", 6),
     ("finish", 5),
-    ("gather", 6),
-    ("compute", 6),
     ("forward", 7),
+    ("compute", 6, 0),
+    ("compute", 6, 1),
     ("send", 6),
+    ("forward", 8),
     ("gather", 7),
-    ("compute", 7),
+    ("gather", 8),
+    TICK,
+    ("compute", 7, 0),
     ("pass", 6),
-    ("forward", 8),
-    ("gather", 8),
+    TICK,
+    ("compute", 8, 0),
+    TICK,
+    ("compute", 8, 1),
+    ("compute", 7, 1),
     TICK,
     ("send", 7),
+    TICK,
+    ("send", 8),
+    ("finish", 6),
+    TICK,
+    ("pass", 8),
+    *[TICK] * 2,
     ("pass", 7),
     TICK,
-    ("finish", 6),
-    TICK,
-    ("compute", 8),
+    ("forward", 9),
+    ("finish", 8),
+    TICK,
+    ("gather", 9),
+    TICK,
+    ("finish", 7),
+    TICK,
+    ("forward", 11),
+    TICK,
+    ("compute", 9, 0),
+    TICK,
+    ("forward", 10),
+    ("compute", 9, 1),
+    TICK,
+    ("gather", 11),
+    ("gather", 10),
+    ("compute", 10, 0),
+    TICK,
+    ("compute", 10, 1),
+    TICK,
+    ("compute", 11, 0),
+    TICK,
+    ("compute", 11, 1),
+    TICK,
+    ("compute", 10, 2),
+    ("send", 10),
+    TICK,
+    ("pass", 10),
+    TICK,
+    ("compute", 9, 2),
+    ("send", 9),
     *[TICK] * 2,
-    ("finish", 7),
-    ("send", 8),
-    ("forward", 9),
-    TICK,
-    ("gather", 9),
-    ("pass", 8),
-    TICK,
-    ("compute", 9),
-    TICK,
-    ("forward", 10),
-    TICK,
-    ("finish", 8),
-    ("send", 9),
-    TICK,
-    ("gather", 10),
+    ("compute", 11, 2),
+    TICK,
     ("pass", 9),
     TICK,
-    ("compute", 10),
-    ("send", 10),
-    TICK,
-    ("forward", 11),
-    ("pass", 10),
-    TICK,
-    ("gather", 11),
-    ("compute", 11),
-    TICK,
     ("send", 11),
     TICK,
     ("pass", 11),
-    *[TICK] * 4,
+    ("finish", 10),
     ("finish", 9),
-    ("finish", 10),
     *[TICK] * 2,
     ("finish", 11),
-    TICK,
 )
 
 
@@ -538,8 +555,9 @@
         v = dot(tokens, wq[2]) + vec_ref[7:8, head_cols : 2 * head_cols]
         qkv[s, 2] = v.astype(LOW)
         keys_valid = lax.broadcasted_iota(jnp.int32, (rows, rows), 0) < lengths_ref[0, s]
-        for j in range(pairs):
-            cols = slice(j * 128, (j + 1) * 128)
+
+        def pair(j, carry):
+            cols = pl.ds(pl.multiple_of(j * 128, 128), 128)
             q, k, v = qkv[s, 0, :, cols], qkv[s, 1, :, cols], qkv[s, 2, :, cols]
             context = jnp.zeros((128, rows), F32)
             for h in range(2):
@@ -550,23 +568,36 @@
                 pt[s, 2 * j + h] = p
                 context = context + dot(masked(v, h).T, p)
             cc[s, :, cols] = context.T.astype(LOW)
-        context = cc[s]
-        for j in range(width // TILE):
-            put_part(s, j, dot(context, wo[:, j * TILE : (j + 1) * TILE]))
+            return carry
+
+        lax.fori_loop(0, pairs, pair, 0)
+
+        def out(j, carry):
+            cols = pl.ds(pl.multiple_of(j * TILE, TILE), TILE)
+            put_part(s, j, dot(cc[s], wo[:, cols]))
+            return carry
+
+        lax.fori_loop(0, width // TILE, out, 0)
 
     def compute_c(s):
-        normed = whole(ua, s)
-        for j in range(hidden // TILE):
-            cols = slice(j * TILE, (j + 1) * TILE)
-            h = dot(normed, wu[:, cols]) + vec_ref[6:7, cols]
+        def tile(j, carry):
+            cols = pl.ds(pl.multiple_of(j * TILE, TILE), TILE)
+            h = dot(whole(ua, s), wu[:, cols]) + vec_ref[6:7, cols]
             phi, density = gelu_parts(h)
             act[s, :, cols] = (h * phi).astype(LOW)
             gp[s, :, cols] = (phi + h * density).astype(LOW)
-        activated = act[s]
-        for j in range(width // TILE):
-            put_part(s, j, dot(activated, wd[:, j * TILE : (j + 1) * TILE]))
-
-    def compute_e(s):
+            return carry
+
+        lax.fori_loop(0, hidden // TILE, tile, 0)
+
+        def down(j, carry):
+            cols = pl.ds(pl.multiple_of(j * TILE, TILE), TILE)
+            put_part(s, j, dot(act[s], wd[:, cols]))
+            return carry
+
+        lax.fori_loop(0, width // TILE, down, 0)
+
+    def compute_e_hidden(s):
         def tile(j, carry):
             cols = pl.ds(pl.multiple_of(j * TILE, TILE), TILE)
             gh = gp[s, :, cols].astype(F32) * dot(whole(g2a, s), wd[cols, :], 1, 1)
@@ -576,6 +607,7 @@
 
         lax.fori_loop(0, hidden // TILE, tile, 0)
 
+    def compute_e_back(s):
         def back(j, carry):
             rows_at = pl.ds(pl.multiple_of(j * TILE, TILE), TILE)
             put_part(s, j, dot(gp[s], wu[rows_at, :], 1, 1))
@@ -583,35 +615,39 @@
 
         lax.fori_loop(0, width // TILE, back, 0)
 
-    def compute_g(s):
+    def head_pair_back(s, j):
+        cols = slice(j * 128, (j + 1) * 128)
+        q, k, v = qkv[s, 0, :, cols], qkv[s, 1, :, cols], qkv[s, 2, :, cols]
+        gc = grads[:, cols]
+        dq = jnp.zeros((128, rows), F32)
+        dk = jnp.zeros((rows, 128), F32)
+        dv = jnp.zeros((rows, 128), F32)
+        for h in range(2):
+            gc_h = masked(gc, h)
+            p = pt[s, 2 * j + h]
+            wide = p.astype(F32)
+            product = wide * dot(v, gc_h, 1, 1)
+            ds = (product - wide * row_sum(product)).astype(LOW)
+            dv = dv + dot(p, gc_h)
+            dk = dk + dot(ds, masked(q, h))
+            dq = dq + dot(masked(k, h).T, ds)
+        dq = dq.T * (HD ** (-0.5))
+        vg[7:8, cols] += row_sum(dq)
+        vg[7:8, head_cols + j * 128 : head_cols + (j + 1) * 128] += row_sum(dv)
+        qkv[s, 0, :, cols] = dq.astype(LOW)
+        qkv[s, 1, :, cols] = dk.astype(LOW)
+        qkv[s, 2, :, cols] = dv.astype(LOW)
+
+    def compute_g_first(s):
         grads[...] = dot(whole(g1a, s), wo[...], 1, 1).astype(LOW)
-
-        def pair(j, carry):
-            cols = pl.ds(pl.multiple_of(j * 128, 128), 128)
-            q, k, v = qkv[s, 0, :, cols], qkv[s, 1, :, cols], qkv[s, 2, :, cols]
-            gc = grads[:, cols]
-            dq = jnp.zeros((128, rows), F32)
-            dk = jnp.zeros((rows, 128), F32)
-            dv = jnp.zeros((rows, 128), F32)
-            for h in range(2):
-                gc_h = masked(gc, h)
-                p = pt[s, 2 * j + h]
-                wide = p.astype(F32)
-                product = wide * dot(v, gc_h, 1, 1)
-                ds = (product - wide * row_sum(product)).astype(LOW)
-                dv = dv + dot(p, gc_h)
-                dk = dk + dot(ds, masked(q, h))
-                dq = dq + dot(masked(k, h).T, ds)
-            dq = dq.T * (HD ** (-0.5))
-            vg[7:8, cols] += row_sum(dq)
-            vg[7:8, pl.ds(pl.multiple_of(head_cols + j * 128, 128), 128)] += row_sum(dv)
-            qkv[s, 0, :, cols] = dq.astype(LOW)
-            qkv[s, 1, :, cols] = dk.astype(LOW)
-            qkv[s, 2, :, cols] = dv.astype(LOW)
-            return carry
-
-        lax.fori_loop(0, pairs, pair, 0)
-
+        for j in range(pairs // 2):
+            head_pair_back(s, j)
+
+    def compute_g_second(s):
+        for j in range(pairs // 2, pairs):
+            head_pair_back(s, j)
+
+    def compute_g_back(s):
         def back(j, carry):
             at = pl.ds(pl.multiple_of(j * TILE, TILE), TILE)
             total = dot(qkv[s, 0], wq[0, at, :], 1, 1)
@@ -622,7 +658,12 @@
 
         lax.fori_loop(0, width // TILE, back, 0)
 
-    computes = (compute_a, compute_c, compute_e, compute_g)
+    computes = (
+        (compute_a,),
+        (compute_c,),
+        (compute_e_hidden, compute_e_back),
+        (compute_g_first, compute_g_second, compute_g_back),
+    )
 
     def reduced(p, s):
         rs_y(p, s).wait()
@@ -706,14 +747,15 @@
     pieces = early_pieces + 1 + 3
 
     def piece(d):
-        if d < down_pieces:
-            cols = slice(d * TILE, (d + 1) * TILE)
-            product = dot(tall(act[:, :, cols]), tall(g2a[...]), 0, 0)
-        elif d < early_pieces:
-            cols = slice((d - down_pieces) * TILE, (d - down_pieces + 1) * TILE)
-            product = dot(tall(ua[:, :, :, cols]), tall(gp[...]), 0, 0)
+        if d < early_pieces:
+            if d < down_pieces:
+                cols = slice(d * TILE, (d + 1) * TILE)
+                left, right = tall(act[:, :, cols]), g2a
+            else:
+                cols = slice((d - down_pieces) * TILE, (d - down_pieces + 1) * TILE)
+                left, right = tall(ua[:, :, :, cols]), gp
         elif d == early_pieces:
-            product = dot(tall(cc[...]), tall(g1a[...]), 0, 0)
+            left, right = tall(cc[...]), g1a
         else:
             right = tall(qkv[:, d - early_pieces - 1])
             for j in range(per_piece):
@@ -724,9 +766,18 @@
                         h * UNIT : (h + 1) * UNIT
                     ].reshape(2, UNIT // 2, head_cols)
             return
-        product = product.astype(LOW)
-        for u in range(per_piece):
-            gb[d * per_piece + u] = product[u * UNIT : (u + 1) * UNIT].reshape(2, UNIT // 2, width)
+
+        def half(j, carry):
+            cols = pl.ds(pl.multiple_of(j * (width // 2), width // 2), width // 2)
+            columns = right[:, :, cols] if len(right.shape) == 3 else right[:, :, :, cols]
+            product = dot(left, tall(columns), 0, 0).astype(LOW)
+            for u in range(per_piece):
+                gb[d * per_piece + u, :, :, cols] = product[u * UNIT : (u + 1) * UNIT].reshape(
+                    2, UNIT // 2, width // 2
+                )
+            return carry
+
+        lax.fori_loop(0, 2, half, 0)
 
     def unit_stores(i, src):
         def make(n, src, dst):
@@ -777,7 +828,8 @@
 
     def step(s, carry, p):
         gathered(p, s)
-        computes[p](s)
+        for compute in computes[p]:
+            compute(s)
         send_sums(p, s)
         pass_sums(p, s)
         if p > 0:
@@ -827,14 +879,14 @@
 
     actions = {
         "gather": gathered,
-        "compute": lambda p, s: computes[p](s),
+        "compute": lambda p, s, part: computes[p][part](s),
         "send": send_sums,
         "pass": pass_sums,
         "finish": lambda p, s: finishes[p](s),
         "forward": forward_block,
     }
     last = PHASES * batches - 1
-    vectors_wait = {("compute", last), ("finish", last - 1)}
+    vectors_wait = {("compute", last, 1), ("finish", last - batches)}
     for action in SCHEDULE:
         if action == TICK:
             if summed:
@@ -842,8 +894,8 @@
                     vector_hop()
                 tick()
         else:
-            name, index = action
-            actions[name](index // batches, index % batches)
+            name, index, *which = action
+            actions[name](index // batches, index % batches, *which)
             vectors_wait.discard(action)
     if summed:
         while tick():

time: 240 us -> 234 us (0.975)
  Pallas kernels: 239 us -> 233 us
    pallas_call x1, Pallas kernels: 231 us -> 224 us  [run_layer(): pl.pallas_call(functools.partial(layer_kernel, summed=summed), out_shape=...]
where the time goes in v1:
time: 234 us
  Pallas kernels  233 us (100%)
    pallas_call x1, Pallas kernels, run_layer(): pl.pallas_call(functools.partial(layer_kernel, summed=summed), out_shape=...  224 us
    pallas_call x1, Pallas kernels, widen(): pl.pallas_call(widen_kernel, out_shape=(*map(as_wide, (down, up, out, qkv...  8.65 us

profile of v1, /device:TPU:0, one launch (start us, length us, event | category | flops | bytes accessed | tf_op | source)
XLA Modules:
  0.0 233.9 jit_solution(5903652291178994483)
XLA Ops:
  0.7 224.4 %layer.1 = (bf16[3,128,1024]{2,1,0:T(8,128)(2,1)}, bf16[3,128,1024]{2,1,0:T(8,128)(2,1)}, bf16[16,2,32,1024]{3,2,1,0:T(8,128)(2,1)}, bf16[16,2,32,1024]{3,2,1,0:...) custom-call(s32[1,3]{1,0:T(1,128)} %lengths_ref.1, ...), custom_call_target="tpu_custom_call" | custom-call | tf_op jit(solution)/shard_map/layer/pallas_call | solution.py:986
  225.1 8.7 %widen.1 = (f32[1024,1024]{1,0:T(8,128)}, f32[1024,1024]{1,0:T(8,128)}, f32[256,1024]{1,0:T(8,128)}, f32[3,1024,256]{2,1,0:T(8,128)}, f32[256]{0:T(256)}, /*inde...) custom-call(bf16[1024,1024]{1,0:T(8,128)(2,1)} %bitcast.10, ...), custom_call_target="tpu_custom_call" | custom-call | tf_op jit(solution)/shard_map/widen/pallas_call | solution.py:1054

commit v2 on v1

--- a/solution.py
+++ b/solution.py
@@ -47,6 +47,7 @@
 SHORT_RING = 8
 STAGE_AT = (0, 1, 2, 3, 4, 6)
 STORE_TICKS = 3
+LOADS_AHEAD = 16
 TICK = ("tick", 0)
 SCHEDULE = (
     ("gather", 6),
@@ -367,22 +368,22 @@
 
 
 def layer_kernel(
-    lengths_ref,
+    lengths_in,
     x_ref,
     cot_ref,
     wqkv_ref,
     wout_ref,
     wup_ref,
     wdown_ref,
-    bout_ref,
-    gain1_ref,
-    bias1_ref,
-    bdown_ref,
-    gain2_ref,
-    bias2_ref,
-    bup_ref,
-    bquery_ref,
-    bvalue_ref,
+    bout_in,
+    gain1_in,
+    bias1_in,
+    bdown_in,
+    gain2_in,
+    bias2_in,
+    bup_in,
+    bquery_in,
+    bvalue_in,
     out_ref,
     gin_ref,
     gdown_ref,
@@ -423,6 +424,7 @@
     vg,
     vec_ref,
     grads,
+    lengths_ref,
     load_sem,
     store_sem,
     agy_send,
@@ -440,7 +442,7 @@
     vec_send,
     vec_recv,
     grad_sem,
-    *,
+    *small_refs,
     summed,
 ):
     batches = x_ref.shape[0]
@@ -523,10 +525,16 @@
     load_cot.start()
 
     vg[...] = jnp.zeros_like(vg)
-    long_refs = (bout_ref, gain1_ref, bias1_ref, bdown_ref, gain2_ref, bias2_ref, bup_ref)
-    for i, ref in enumerate(long_refs):
+    small_ins = (bout_in, gain1_in, bias1_in, bdown_in, gain2_in, bias2_in, bup_in, bquery_in, bvalue_in)
+    small = [load(n + 5, lengths_in, lengths_ref)]
+    small += [load(n + 6 + i, ref, held_ref) for i, (ref, held_ref) in enumerate(zip(small_ins, small_refs))]
+    for cp in small:
+        cp.start()
+    for cp in small:
+        cp.wait()
+    for i, ref in enumerate(small_refs[:7]):
         vec_ref[i : i + 1, :] = ref[...].astype(F32).reshape(1, -1)
-    for i, ref in enumerate((bquery_ref, bvalue_ref)):
+    for i, ref in enumerate(small_refs[7:]):
         vec_ref[7:8, i * head_cols : (i + 1) * head_cols] = ref[...].astype(F32).reshape(1, -1)
     lane = lax.broadcasted_iota(jnp.int32, (rows, 128), 1)
     low_half = lane < HD
@@ -902,7 +910,8 @@
             vector_hop()
         while vector_hop():
             pass
-        vsum_ref[...] = held[VECTOR_HOPS - 1]
+        store_sums = store(2 * batches, held.at[VECTOR_HOPS - 1], vsum_ref)
+        store_sums.start()
     else:
         stores = []
         for d in range(pieces):
@@ -911,11 +920,13 @@
                 stores += unit_stores(i, gb.at[i])
                 for cp in unit_stores(i, gb.at[i]):
                     cp.start()
-        vsum_ref[...] = vg[...]
+        store_sums = store(2 * batches, vg, vsum_ref)
+        store_sums.start()
         for cp in stores:
             cp.wait()
     for s in range(batches):
         store(batches + s, cot.at[s], gin_ref.at[s]).wait()
+    store_sums.wait()
 
     def drain(i, carry):
         for p in range(PHASES):
@@ -938,7 +949,6 @@
     units = down + up + out + 3 * out
     ring, short_ring = (RING, SHORT_RING) if summed else (1, 1)
     any_space = pl.BlockSpec(memory_space=pl.ANY)
-    vmem = pl.BlockSpec(memory_space=pltpu.VMEM)
     dma = pltpu.SemaphoreType.DMA
     low = lambda *shape: pltpu.VMEM(shape, LOW)
     wide = lambda *shape: pltpu.VMEM(shape, F32)
@@ -977,11 +987,13 @@
         wide(8, width),
         wide(8, width),
         low(rows, head_cols),
-        dma((batches + 5,)),
-        dma((2 * batches,)),
+        pltpu.SMEM(lengths.shape, jnp.int32),
+        dma((batches + 15,)),
+        dma((2 * batches + 1,)),
     ]
     scratch += [dma((PHASES, batches))] * 10 + [dma((HOPS, units // 2))] * 2 + [dma((VECTOR_HOPS,))] * 2
     scratch.append(dma((units, TILE // UNIT)))
+    scratch += [low(width)] * 7 + [low(head_cols)] * 2
     low_out = lambda *shape: jax.ShapeDtypeStruct(shape, LOW)
     return pl.pallas_call(
         functools.partial(layer_kernel, summed=summed),
@@ -994,8 +1006,8 @@
             low_out(3, width // UNIT, 2, half, head_cols),
             jax.ShapeDtypeStruct((8, width), F32),
         ),
-        in_specs=[pl.BlockSpec(memory_space=pltpu.SMEM)] + [any_space] * 6 + [vmem] * 9,
-        out_specs=(any_space,) * 6 + (vmem,),
+        in_specs=[any_space] * 16,
+        out_specs=(any_space,) * 7,
         scratch_shapes=scratch,
         compiler_params=pltpu.CompilerParams(
             collective_id=0, has_side_effects=True, vmem_limit_bytes=63 << 20
@@ -1008,7 +1020,8 @@
     down_ref, up_ref, out_ref, qkv_ref, sums_ref, rows_ref, gin_ref,
     down_wide, up_wide, out_wide, qkv_wide, *refs,
 ):
-    vectors, (rows_copy, gin_copy, low, wide, low_qkv, wide_qkv, rows, load_sem, store_sem) = refs[:9], refs[9:]
+    vectors, refs = refs[:9], refs[9:]
+    rows_copy, gin_copy, low, wide, low_qkv, wide_qkv, rows, sums, load_sem, store_sem, vec_sem, *made_vectors = refs
     work = []
 
     def part(src, dst, held, made):
@@ -1027,25 +1040,37 @@
     for i, (src, dst) in enumerate(((rows_ref, rows_copy), (gin_ref, gin_copy))):
         block = rows.at[i]
         part(src, dst, block, block)
-    for get, _, _, _ in work:
+    load_sums = pltpu.make_async_copy(sums_ref, sums, vec_sem.at[0])
+    for get, _, _, _ in work[:LOADS_AHEAD]:
         get.start()
-    head_cols = vectors[0].shape[0]
-    vectors[0][...] = sums_ref[7, :head_cols]
-    vectors[1][...] = sums_ref[7, head_cols : 2 * head_cols]
-    for ref, row in zip(vectors[2:], (0, 1, 2, 6, 3, 4, 5)):
-        ref[...] = sums_ref[row]
-    for get, held, made, put in work:
+    load_sums.start()
+    for n, (get, held, made, put) in enumerate(work):
         get.wait()
+        if n + LOADS_AHEAD < len(work):
+            work[n + LOADS_AHEAD][0].start()
         if made is not held:
             made[...] = held[...].astype(F32)
         put.start()
+    load_sums.wait()
+    head_cols = out_ref.shape[0]
+    for i in range(2):
+        made_vectors[i][...] = sums[7, i * head_cols : (i + 1) * head_cols]
+    for ref, row in zip(made_vectors[2:], (0, 1, 2, 6, 3, 4, 5)):
+        ref[...] = sums[row]
+    puts = [
+        pltpu.make_async_copy(src, dst, vec_sem.at[1 + i])
+        for i, (src, dst) in enumerate(zip(made_vectors, vectors))
+    ]
+    for cp in puts:
+        cp.start()
+    for cp in puts:
+        cp.wait()
     for _, _, _, put in work:
         put.wait()
 
 
 def widen(down, up, out, qkv, sums, rows, gin):
     any_space = pl.BlockSpec(memory_space=pl.ANY)
-    vmem = pl.BlockSpec(memory_space=pltpu.VMEM)
     dma = pltpu.SemaphoreType.DMA
     width = down.shape[1]
     pieces = (down.shape[0] + up.shape[0] + out.shape[0]) // TILE
@@ -1060,16 +1085,20 @@
             jax.ShapeDtypeStruct(rows.shape, rows.dtype),
             jax.ShapeDtypeStruct(gin.shape, gin.dtype),
         ),
-        in_specs=[any_space] * 4 + [vmem] + [any_space] * 2,
-        out_specs=(any_space,) * 4 + (vmem,) * 9 + (any_space,) * 2,
+        in_specs=[any_space] * 7,
+        out_specs=(any_space,) * 15,
         scratch_shapes=[
             pltpu.VMEM((pieces, TILE, width), LOW),
             pltpu.VMEM((pieces, TILE, width), F32),
             pltpu.VMEM(qkv.shape, LOW),
             pltpu.VMEM(qkv.shape, F32),
             pltpu.VMEM((2, *rows.shape), LOW),
+            pltpu.VMEM(sums.shape, F32),
             dma((pieces + 5,)),
             dma((pieces + 5,)),
+            dma((10,)),
+            *[pltpu.VMEM((out.shape[0],), F32)] * 2,
+            *[pltpu.VMEM((width,), F32)] * 7,
         ],
         compiler_params=pltpu.CompilerParams(vmem_limit_bytes=62 << 20),
         name="widen",

time: 234 us -> 232 us (level)
  no operation moved by 1% of the time
where the time goes in v2:
time: 232 us
  Pallas kernels  231 us (100%)
    pallas_call x1, Pallas kernels, run_layer(): pl.pallas_call(functools.partial(layer_kernel, summed=summed), out_shape=...  224 us
    pallas_call x1, Pallas kernels, widen(): pl.pallas_call(widen_kernel, out_shape=(*map(as_wide, (down, up, out, qkv...  7.36 us

profile of v2, /device:TPU:0, one launch (start us, length us, event | category | flops | bytes accessed | tf_op | source)
XLA Modules:
  0.0 232.1 jit_solution(15920123973260651355)
XLA Ops:
  0.7 223.9 %layer.1 = (bf16[3,128,1024]{2,1,0:T(8,128)(2,1)}, bf16[3,128,1024]{2,1,0:T(8,128)(2,1)}, bf16[16,2,32,1024]{3,2,1,0:T(8,128)(2,1)}, bf16[16,2,32,1024]{3,2,1,0:...) custom-call(s32[1,3]{1,0:T(1,128)} %lengths_in.1, ...), custom_call_target="tpu_custom_call" | custom-call | tf_op jit(solution)/shard_map/layer/pallas_call | solution.py:998
  224.5 7.4 %widen.1 = (f32[1024,1024]{1,0:T(8,128)}, f32[1024,1024]{1,0:T(8,128)}, f32[256,1024]{1,0:T(8,128)}, f32[3,1024,256]{2,1,0:T(8,128)}, f32[256]{0:T(256)}, /*inde...) custom-call(bf16[1024,1024]{1,0:T(8,128)(2,1)} %bitcast.10, ...), custom_call_target="tpu_custom_call" | custom-call | tf_op jit(solution)/shard_map/widen/pallas_call | solution.py:1079

commit v3 on v2

--- a/solution.py
+++ b/solution.py
@@ -787,29 +787,18 @@
 
         lax.fori_loop(0, 2, half, 0)
 
-    def unit_stores(i, src):
-        def make(n, src, dst):
-            return pltpu.make_async_copy(src, dst, grad_sem.at[i, n])
-
-        if i < down_pieces * per_piece:
-            return [make(0, src, gdown_ref.at[i])]
-        i_up = i - down_pieces * per_piece
-        if i_up < up_pieces * per_piece:
-            return [make(0, src, gup_ref.at[i_up])]
-        i_out = i - early_pieces * per_piece
-        if i_out < per_piece:
-            return [make(0, src, gout_ref.at[i_out])]
-        i_qkv = i_out - per_piece
-        kind, j = i_qkv // per_piece, i_qkv % per_piece
-        return [
-            make(h, src.at[:, :, pl.ds(h * head_cols, head_cols)], gqkv_ref.at[kind, j * per_piece + h])
-            for h in range(per_piece)
-        ]
+    def unit_store(i, src):
+        at = i
+        for ref in (gdown_ref, gup_ref, gout_ref, gqkv_ref):
+            if at < ref.shape[0]:
+                break
+            at -= ref.shape[0]
+        return pltpu.make_async_copy(src, ref.at[at], grad_sem.at[i])
 
     unit_pairs = pieces * per_piece // 2
 
     def pair_stores(k):
-        return unit_stores(2 * k, rx.at[k % RING]) + unit_stores(2 * k + 1, rb.at[k % RING])
+        return unit_store(2 * k, rx.at[k % RING]), unit_store(2 * k + 1, rb.at[k % RING])
 
     ticks = iter(range(-1, unit_pairs + STAGE_AT[-1] + STORE_TICKS + 1))
 
@@ -817,10 +806,6 @@
         now = next(ticks, None)
         if now is None:
             return False
-        if 0 <= now - STAGE_AT[-1] - STORE_TICKS < unit_pairs:
-            reducer.drain(now - STAGE_AT[-1] - STORE_TICKS)
-            for cp in pair_stores(now - STAGE_AT[-1] - STORE_TICKS):
-                cp.wait()
         k = now + 1
         if k < unit_pairs:
             if 2 * k % per_piece == 0:
@@ -832,6 +817,10 @@
         if 0 <= now - STAGE_AT[-1] < unit_pairs:
             for cp in pair_stores(now - STAGE_AT[-1]):
                 cp.start()
+        if 0 <= now - STAGE_AT[-1] - STORE_TICKS < unit_pairs:
+            reducer.drain(now - STAGE_AT[-1] - STORE_TICKS)
+            for cp in pair_stores(now - STAGE_AT[-1] - STORE_TICKS):
+                cp.wait()
         return True
 
     def step(s, carry, p):
@@ -917,9 +906,8 @@
         for d in range(pieces):
             piece(d)
             for i in range(d * per_piece, (d + 1) * per_piece):
-                stores += unit_stores(i, gb.at[i])
-                for cp in unit_stores(i, gb.at[i]):
-                    cp.start()
+                stores.append(unit_store(i, gb.at[i]))
+                stores[-1].start()
         store_sums = store(2 * batches, vg, vsum_ref)
         store_sums.start()
         for cp in stores:
@@ -992,7 +980,7 @@
         dma((2 * batches + 1,)),
     ]
     scratch += [dma((PHASES, batches))] * 10 + [dma((HOPS, units // 2))] * 2 + [dma((VECTOR_HOPS,))] * 2
-    scratch.append(dma((units, TILE // UNIT)))
+    scratch.append(dma((units,)))
     scratch += [low(width)] * 7 + [low(head_cols)] * 2
     low_out = lambda *shape: jax.ShapeDtypeStruct(shape, LOW)
     return pl.pallas_call(
@@ -1003,7 +991,7 @@
             low_out(down, 2, half, width),
             low_out(up, 2, half, hidden),
             low_out(out, 2, half, width),
-            low_out(3, width // UNIT, 2, half, head_cols),
+            low_out(3 * out, 2, half, width),
             jax.ShapeDtypeStruct((8, width), F32),
         ),
         in_specs=[any_space] * 16,
@@ -1037,6 +1025,7 @@
             i += 1
     for i in range(3):
         part(qkv_ref.at[i], qkv_wide.at[i], low_qkv.at[i], wide_qkv.at[i])
+    fold = low_qkv.shape[3] // wide_qkv.shape[2]
     for i, (src, dst) in enumerate(((rows_ref, rows_copy), (gin_ref, gin_copy))):
         block = rows.at[i]
         part(src, dst, block, block)
@@ -1048,7 +1037,13 @@
         get.wait()
         if n + LOADS_AHEAD < len(work):
             work[n + LOADS_AHEAD][0].start()
-        if made is not held:
+        if len(held.shape) == 3 and made is not held:
+            cols = made.shape[1]
+            for j in range(held.shape[0]):
+                for h in range(fold):
+                    at = (j * fold + h) * UNIT
+                    made[at : at + UNIT, :] = held[j, :, h * cols : (h + 1) * cols].astype(F32)
+        elif made is not held:
             made[...] = held[...].astype(F32)
         put.start()
     load_sums.wait()
@@ -1079,7 +1074,8 @@
     return pl.pallas_call(
         widen_kernel,
         out_shape=(
-            *map(as_wide, (down, up, out, qkv)),
+            *map(as_wide, (down, up, out)),
+            jax.ShapeDtypeStruct((3, width, out.shape[0]), F32),
             *[vector(out.shape[0])] * 2,
             *[vector(width)] * 7,
             jax.ShapeDtypeStruct(rows.shape, rows.dtype),
@@ -1091,7 +1087,7 @@
             pltpu.VMEM((pieces, TILE, width), LOW),
             pltpu.VMEM((pieces, TILE, width), F32),
             pltpu.VMEM(qkv.shape, LOW),
-            pltpu.VMEM(qkv.shape, F32),
+            pltpu.VMEM((3, width, out.shape[0]), F32),
             pltpu.VMEM((2, *rows.shape), LOW),
             pltpu.VMEM(sums.shape, F32),
             dma((pieces + 5,)),
@@ -1147,7 +1143,7 @@
         grad_down.reshape(hidden, width),
         grad_up.reshape(width, hidden),
         grad_out.reshape(head_cols, width),
-        grad_qkv.reshape(3, width, head_cols),
+        grad_qkv.reshape(3, -1, UNIT, width),
         sums,
         output,
         grad_inputs,

time: 232 us -> 231 us (level)
  no operation moved by 1% of the time
where the time goes in v3:
time: 231 us
  Pallas kernels  230 us (100%)
    pallas_call x1, Pallas kernels, run_layer(): pl.pallas_call(functools.partial(layer_kernel, summed=summed), out_shape=...  223 us
    pallas_call x1, Pallas kernels, widen(): pl.pallas_call(widen_kernel, out_shape=(*map(as_wide, (down, up, out)), j...  7.36 us

profile of v3, /device:TPU:0, one launch (start us, length us, event | category | flops | bytes accessed | tf_op | source)
XLA Modules:
  0.0 230.8 jit_solution(6639859838947886966)
XLA Ops:
  0.7 222.6 %layer.1 = (bf16[3,128,1024]{2,1,0:T(8,128)(2,1)}, bf16[3,128,1024]{2,1,0:T(8,128)(2,1)}, bf16[16,2,32,1024]{3,2,1,0:T(8,128)(2,1)}, bf16[16,2,32,1024]{3,2,1,0:...) custom-call(s32[1,3]{1,0:T(1,128)} %lengths_in.1, ...), custom_call_target="tpu_custom_call" | custom-call | tf_op jit(solution)/shard_map/layer/pallas_call | solution.py:986
  223.2 7.4 %widen.1 = (f32[1024,1024]{1,0:T(8,128)}, f32[1024,1024]{1,0:T(8,128)}, f32[256,1024]{1,0:T(8,128)}, f32[3,1024,256]{2,1,0:T(8,128)}, f32[256]{0:T(256)}, /*inde...) custom-call(bf16[1024,1024]{1,0:T(8,128)(2,1)} %bitcast.10, ...), custom_call_target="tpu_custom_call" | custom-call | tf_op jit(solution)/shard_map/widen/pallas_call | solution.py:1074

commit v4 on v3

--- a/solution.py
+++ b/solution.py
@@ -135,6 +135,7 @@
         self.to_x = {"dp": self.z * 2 + (1 - self.x)}
         self.to_pair = {"dp": (self.z + 1 - 2 * self.side) * 2 + self.x}
         self.to_mid = {"dp": (3 - self.z) * 2 + self.x}
+        self.inside = None
         self.gb, self.rx, self.rz, self.rm, self.rb, self.rn, self.rq = gb, rx, rz, rm, rb, rn, rq
         self.send_sems, self.recv_sems = send_sems, recv_sems
 
@@ -147,14 +148,24 @@
         for device in (self.to_x, self.to_pair) + tuple(extra):
             signal(device)
 
-        @pl.when(self.inner)
+        @self.when(True)
         def _():
             signal(self.to_mid)
             pl.semaphore_wait(barrier, 3 + len(extra))
 
-        @pl.when(self.outer)
+        @self.when(False)
         def _():
             pl.semaphore_wait(barrier, 2 + len(extra))
+
+    def when(self, inner):
+        if self.inside is None:
+            return pl.when(self.inner if inner else self.outer)
+
+        def run(step):
+            if inner == self.inside:
+                step()
+
+        return run
 
     def copy(self, hop, k, src, dst, device):
         return pltpu.make_async_remote_copy(
@@ -205,7 +216,7 @@
     def start(self, k):
         self.ax(k).start()
 
-        @pl.when(self.outer)
+        @self.when(False)
         def _():
             self.bi(k).start()
 
@@ -214,12 +225,12 @@
         own = self.gb.at[2 * k, self.x]
         self.add(own, own, self.rx.at[k % RING, self.x])
 
-        @pl.when(self.outer)
+        @self.when(False)
         def _():
             self.az(k).start()
 
     def stage2(self, k):
-        @pl.when(self.inner)
+        @self.when(True)
         def _():
             self.bi(k).wait_recv()
             away = self.gb.at[2 * k + 1, 1 - self.m]
@@ -233,7 +244,7 @@
             self.am(k).start()
 
     def stage3(self, k):
-        @pl.when(self.inner)
+        @self.when(True)
         def _():
             self.bm(k).wait()
             own = self.gb.at[2 * k + 1, self.m]
@@ -245,20 +256,20 @@
             self.ag(k).start()
 
     def stage4(self, k):
-        @pl.when(self.inner)
+        @self.when(True)
         def _():
             self.bx(k).wait()
             self.add(self.rb.at[k % RING, self.m], self.gb.at[2 * k + 1, self.m], self.rq.at[k % SHORT_RING])
             self.bg(k).start()
             self.bo(k).start()
 
-        @pl.when(self.outer)
+        @self.when(False)
         def _():
             self.ao(k).wait_recv()
             self.ag(k).start()
 
     def stage5(self, k):
-        @pl.when(self.inner)
+        @self.when(True)
         def _():
             self.bg(k).wait_recv()
             self.bp(k).start()
@@ -266,7 +277,7 @@
         self.ag(k).wait_recv()
 
     def stage6(self, k):
-        @pl.when(self.outer)
+        @self.when(False)
         def _():
             self.bo(k).wait_recv()
             self.bp(k).wait_recv()
@@ -274,14 +285,14 @@
     def drain(self, k):
         self.ag(k).wait_send()
 
-        @pl.when(self.inner)
+        @self.when(True)
         def _():
             self.ao(k).wait_send()
             self.bg(k).wait_send()
             self.bo(k).wait_send()
             self.bp(k).wait_send()
 
-        @pl.when(self.outer)
+        @self.when(False)
         def _():
             self.az(k).wait_send()
             self.bi(k).wait_send()
@@ -807,20 +818,32 @@
         if now is None:
             return False
         k = now + 1
-        if k < unit_pairs:
-            if 2 * k % per_piece == 0:
-                piece(2 * k // per_piece)
-            reducer.start(k)
-        for stage, at in zip(reducer.stages, STAGE_AT):
-            if 0 <= now - at < unit_pairs:
-                stage(reducer, now - at)
-        if 0 <= now - STAGE_AT[-1] < unit_pairs:
-            for cp in pair_stores(now - STAGE_AT[-1]):
-                cp.start()
-        if 0 <= now - STAGE_AT[-1] - STORE_TICKS < unit_pairs:
-            reducer.drain(now - STAGE_AT[-1] - STORE_TICKS)
-            for cp in pair_stores(now - STAGE_AT[-1] - STORE_TICKS):
-                cp.wait()
+        if k < unit_pairs and 2 * k % per_piece == 0:
+            piece(2 * k // per_piece)
+
+        def serve():
+            if k < unit_pairs:
+                reducer.start(k)
+            for stage, at in zip(reducer.stages, STAGE_AT):
+                if 0 <= now - at < unit_pairs:
+                    stage(reducer, now - at)
+            if 0 <= now - STAGE_AT[-1] < unit_pairs:
+                for cp in pair_stores(now - STAGE_AT[-1]):
+                    cp.start()
+            old = now - STAGE_AT[-1] - STORE_TICKS
+            if 0 <= old < unit_pairs:
+                reducer.drain(old)
+                for cp in pair_stores(old):
+                    cp.wait()
+
+        for inside in (True, False):
+            reducer.inside = inside
+
+            @pl.when(reducer.inner if inside else reducer.outer)
+            def _():
+                serve()
+
+        reducer.inside = None
         return True
 
     def step(s, carry, p):
@@ -894,6 +917,15 @@
             name, index, *which = action
             actions[name](index // batches, index % batches, *which)
             vectors_wait.discard(action)
+    def drain(i, carry):
+        for p in range(PHASES):
+            ag_y(p, i, t).wait_send()
+            ag_c(p, i, t).wait_send()
+            ag_f(p, i, t_y).wait_send()
+        return carry
+
+    lax.fori_loop(0, batches, drain, 0)
+
     if summed:
         while tick():
             vector_hop()
@@ -915,15 +947,6 @@
     for s in range(batches):
         store(batches + s, cot.at[s], gin_ref.at[s]).wait()
     store_sums.wait()
-
-    def drain(i, carry):
-        for p in range(PHASES):
-            ag_y(p, i, t).wait_send()
-            ag_c(p, i, t).wait_send()
-            ag_f(p, i, t_y).wait_send()
-        return carry
-
-    lax.fori_loop(0, batches, drain, 0)
 
 
 def run_layer(lengths, x, cot, wqkv, wout, wup, wdown, vectors, summed):

time: 231 us -> 231 us (level)
  no operation moved by 1% of the time
where the time goes in v4:
time: 231 us
  Pallas kernels  230 us (100%)
    pallas_call x1, Pallas kernels, run_layer(): pl.pallas_call(functools.partial(layer_kernel, summed=summed), out_shape=...  223 us
    pallas_call x1, Pallas kernels, widen(): pl.pallas_call(widen_kernel, out_shape=(*map(as_wide, (down, up, out)), j...  7.36 us

profile of v4, /device:TPU:0, one launch (start us, length us, event | category | flops | bytes accessed | tf_op | source)
XLA Modules:
  0.0 230.7 jit_solution(8201785637591804891)
XLA Ops:
  0.7 222.5 %layer.1 = (bf16[3,128,1024]{2,1,0:T(8,128)(2,1)}, bf16[3,128,1024]{2,1,0:T(8,128)(2,1)}, bf16[16,2,32,1024]{3,2,1,0:T(8,128)(2,1)}, bf16[16,2,32,1024]{3,2,1,0:...) custom-call(s32[1,3]{1,0:T(1,128)} %lengths_in.1, ...), custom_call_target="tpu_custom_call" | custom-call | tf_op jit(solution)/shard_map/layer/pallas_call | solution.py:1009
  223.2 7.4 %widen.1 = (f32[1024,1024]{1,0:T(8,128)}, f32[1024,1024]{1,0:T(8,128)}, f32[256,1024]{1,0:T(8,128)}, f32[3,1024,256]{2,1,0:T(8,128)}, f32[256]{0:T(256)}, /*inde...) custom-call(bf16[1024,1024]{1,0:T(8,128)(2,1)} %bitcast.10, ...), custom_call_target="tpu_custom_call" | custom-call | tf_op jit(solution)/shard_map/widen/pallas_call | solution.py:1097
